TPU v7x, 256 devices: a whole 4x4x8 slice. The times are simulated.
256 devices in a mesh: pipe: 4 (over x), seq: 32 (over z, y), batch: 2 (over core).
Axes of the slice: x: 4, y: 4, z: 8, core: 2. Of those that a mesh axis runs over, the one named last changes fastest.
Arguments:
- latent_noise: float32 [4, 2, 512, 64], P('pipe', 'batch', 'seq'), may hold values from -6 to 6
- text_rows: bfloat16 [4, 2, 256, 4096], P(None, 'batch', None, 'seq'), may hold values from -6 to 6
- text_lengths: int32 [4, 2], P(None, 'batch'), may hold values from 32 to 256, as said below
- plan: int32 [3], replicated, may hold values from 1 to 1000, as said below
- context_weight: bfloat16 [4096, 1536], P('seq'), may hold values from -0.09375 to 0.09375
- w_embed: bfloat16 [64, 1536], replicated, may hold values from -0.75 to 0.75
- w_attention: bfloat16 [4, 1536, 4608], P('pipe', 'batch'), may hold values from -1 to 1
- w_project: bfloat16 [4, 1536, 1536], P('pipe', 'batch'), may hold values from -0.15625 to 0.15625
- w_modulate: bfloat16 [4, 256, 4608], P('pipe', 'batch'), may hold values from -0.375 to 0.375
- w_final: bfloat16 [1536, 64], replicated, may hold values from -0.15625 to 0.15625
Outputs:
- final_latent: float32 [4, 2, 512, 64], P('pipe', 'batch', 'seq')
Inputs may be any that keep to these rules, and one draw needn't show every extreme that they name: `text_lengths`: at least one prompt has 256 live rows and one has 32. `plan`: strictly falling; the first entry is 1000 and the last is 1.
All inputs are finite; a program needn't handle non-finite values.
Results may differ from a plain program's by a relative error of at most 0.02.
Values may be sent and summed in bfloat16 or wider, within the bound.
No kernel may reach another device: no remote copies, remote signals or barrier semaphores. Data moves between devices by JAX's collectives and lax.ppermute only.
A program may use at most 128 MiB of HBM per device.

v0:
```python
import math

import jax
import jax.numpy as jnp
from jax import lax
from jax.sharding import PartitionSpec as P

HEADS = 16
STEPS = 2


epsilon = 1e-06


def shifted(value, axis, by):
    peers = lax.axis_size(axis)
    return lax.ppermute(value, axis, [(i, (i + by) % peers) for i in range(peers)])


def layer_norm(hidden):
    values = hidden.astype(jnp.float32)
    center = values - jnp.mean(values, axis=-1, keepdims=True)
    spread = jnp.mean(center * center, axis=-1, keepdims=True)
    return center * lax.rsqrt(spread + epsilon)


def time_features(noise_level, feature_count):
    half_count = feature_count // 2
    wave_frequency = jnp.exp(
        -math.log(10000.0) * jnp.arange(half_count, dtype=jnp.float32) / half_count
    )
    angles = noise_level * wave_frequency
    return jnp.concatenate([jnp.cos(angles), jnp.sin(angles)]).astype(jnp.bfloat16)


def on_device(
    latent_noise,
    text_rows,
    text_lengths,
    plan,
    context_weight,
    w_embed,
    w_attention,
    w_project,
    w_modulate,
    w_final,
):
    seq_count = lax.axis_size("seq")
    device_count = lax.axis_size("pipe")
    section = lax.axis_index("pipe")
    tokens_here = latent_noise.shape[2]
    text_total = text_rows.shape[2]
    text_here = text_total // seq_count
    model_width = w_embed.shape[1]
    gathered = (
        lax.all_gather(w_attention, "batch", axis=1, tiled=True),
        lax.all_gather(w_project, "batch", axis=1, tiled=True),
        lax.all_gather(w_modulate, "batch", axis=1, tiled=True),
    )
    attn_weight = gathered[0][0]
    proj_weight = gathered[1][0]
    mod_weight = gathered[2][0]
    inner_width = proj_weight.shape[0]
    head_size = inner_width // HEADS
    unit_count = max(HEADS, seq_count)
    replica_count = unit_count // HEADS
    unit_here = unit_count // seq_count
    query_rows = tokens_here // replica_count
    factor = 1.0 / math.sqrt(head_size)
    resident_text = text_rows[:, 0]
    context = lax.psum_scatter(
        jnp.einsum(
            "ipe,ea->pia", resident_text, context_weight, preferred_element_type=jnp.float32
        ),
        "seq",
        scatter_dimension=0,
        tiled=True,
    ).astype(jnp.bfloat16)
    live_text = jnp.arange(text_total)[None, :] < text_lengths[:, 0][:, None]

    def key_units(key_rows):
        row_count = key_rows.shape[0]
        heads_first = key_rows.reshape(row_count, HEADS, head_size).transpose(1, 0, 2)
        return jnp.repeat(heads_first, replica_count, axis=0).reshape(
            unit_count, row_count * head_size
        )

    def query_units(query_block):
        parted = query_block.reshape(replica_count, query_rows, HEADS, head_size).transpose(
            2, 0, 1, 3
        )
        return parted.reshape(unit_count, query_rows * head_size)

    def from_units(blocks):
        parted = blocks.reshape(HEADS, replica_count, query_rows, head_size).transpose(1, 2, 0, 3)
        return parted.reshape(tokens_here, inner_width)

    def split_joined(moved):
        parted = moved.reshape(unit_here, seq_count, tokens_here + text_here, head_size)
        image_part = parted[:, :, :tokens_here].reshape(
            unit_here, seq_count * tokens_here, head_size
        )
        text_part = parted[:, :, tokens_here:].reshape(unit_here, seq_count * text_here, head_size)
        return jnp.concatenate([image_part, text_part], 1)

    text_scale_weight = attn_weight[:, inner_width:]

    def one_turn(turn_index, state_pair):
        hidden, latent = state_pair
        anchor = (section - turn_index) % device_count
        entry_turn = (device_count - anchor) % device_count
        passed = turn_index - entry_turn
        active = (passed >= 0) & (passed < STEPS * device_count)
        step_index = jnp.clip(passed // device_count, 0, STEPS - 1)
        positions = jnp.arange(STEPS + 1)
        noise_level = jnp.sum(jnp.where(positions == step_index, plan, 0)).astype(jnp.float32)
        next_level = jnp.sum(jnp.where(positions == step_index + 1, plan, 0)).astype(jnp.float32)
        features = time_features(noise_level, mod_weight.shape[0])
        modulation = jnp.dot(features[None, :], mod_weight, preferred_element_type=jnp.float32)[0]
        mod_shift = modulation[:model_width]
        mod_scale = modulation[model_width : 2 * model_width]
        mod_gate = modulation[2 * model_width :]
        embedded = jnp.dot(
            latent.astype(jnp.bfloat16), w_embed, preferred_element_type=jnp.float32
        ).astype(jnp.bfloat16)
        incoming = jnp.where(section == 0, embedded, hidden)
        normed = (layer_norm(incoming) * (1.0 + mod_scale) + mod_shift).astype(jnp.bfloat16)
        projected = jnp.dot(normed, attn_weight, preferred_element_type=jnp.float32).astype(
            jnp.bfloat16
        )
        queries = query_units(projected[:, :inner_width])
        image_keys = projected[:, inner_width : 2 * inner_width]
        image_values = projected[:, 2 * inner_width :]
        live_keys = lax.dynamic_index_in_dim(live_text, anchor, 0, keepdims=False)
        context_rows = lax.dynamic_index_in_dim(context, anchor, 1, keepdims=False)
        text_pairs = jnp.dot(
            context_rows, text_scale_weight, preferred_element_type=jnp.float32
        ).astype(jnp.bfloat16)
        joined_keys = jnp.concatenate([image_keys, text_pairs[:, :inner_width]], 0)
        joined_values = jnp.concatenate([image_values, text_pairs[:, inner_width:]], 0)
        got_queries, got_keys, got_values = (
            lax.all_to_all(queries, "seq", split_axis=0, concat_axis=1, tiled=True),
            lax.all_to_all(key_units(joined_keys), "seq", split_axis=0, concat_axis=1, tiled=True),
            lax.all_to_all(
                key_units(joined_values), "seq", split_axis=0, concat_axis=1, tiled=True
            ),
        )
        all_keys = split_joined(got_keys)
        all_values = split_joined(got_values)
        query_heads = got_queries.reshape(unit_here, seq_count * query_rows, head_size)
        scores = (
            jnp.einsum("uqc,ukc->uqk", query_heads, all_keys, preferred_element_type=jnp.float32)
            * factor
        )
        key_mask = jnp.concatenate([jnp.ones((seq_count * tokens_here,), dtype=bool), live_keys])
        scores = jnp.where(key_mask[None, None, :], scores, -1e30)
        highest = jnp.max(scores, axis=-1, keepdims=True)
        exponents = jnp.exp(scores - highest)
        totals = jnp.sum(exponents, axis=-1, keepdims=True)
        weights = (exponents / totals).astype(jnp.bfloat16)
        attended = jnp.einsum(
            "uqk,ukc->uqc", weights, all_values, preferred_element_type=jnp.float32
        ).astype(jnp.bfloat16)
        returned = lax.all_to_all(
            attended.reshape(unit_here, seq_count * query_rows * head_size),
            "seq",
            split_axis=1,
            concat_axis=0,
            tiled=True,
        )
        merged_heads = from_units(returned)
        update = jnp.dot(merged_heads, proj_weight, preferred_element_type=jnp.float32)
        updated = (incoming.astype(jnp.float32) + mod_gate * update).astype(jnp.bfloat16)
        normed_out = layer_norm(updated).astype(jnp.bfloat16)
        velocity = jnp.dot(normed_out, w_final, preferred_element_type=jnp.float32)
        stepped = latent + (next_level - noise_level) / 1000.0 * velocity
        new_latent = jnp.where(active & (section == device_count - 1), stepped, latent)
        new_hidden = jnp.where(active, updated, hidden)
        sent_hidden, sent_latent = (
            shifted(new_hidden.astype(jnp.float32).astype(jnp.bfloat16), "pipe", 1).astype(
                jnp.float32
            ),
            shifted(new_latent.astype(jnp.bfloat16), "pipe", 1).astype(new_latent.dtype),
        )
        return (sent_hidden.astype(jnp.bfloat16), sent_latent)

    start_hidden = jnp.zeros((tokens_here, model_width), jnp.bfloat16)
    final_pair = lax.fori_loop(
        0, device_count * (STEPS + 1), one_turn, (start_hidden, latent_noise[0, 0])
    )
    return final_pair[1].reshape(latent_noise.shape)


def solution(mesh):
    placed = (
        P("pipe", "batch", "seq", None),
        P(None, "batch", None, "seq"),
        P(None, "batch"),
        P(),
        P("seq", None),
        P(),
        P("pipe", "batch", None),
        P("pipe", "batch", None),
        P("pipe", "batch", None),
        P(),
    )
    return jax.shard_map(
        on_device,
        mesh=mesh,
        in_specs=placed,
        out_specs=P("pipe", "batch", "seq", None),
        check_vma=False,
    )
```

profile of v0, /device:TPU:2, one launch (start us, length us, event | category | flops | bytes accessed | tf_op | source)
XLA Modules:
  0.0 1278.9 jit_solution(2273198371216502025)
XLA Ops:
  21.8 184.1 %all-reduce.3 = bf16[256,4,1536]{2,1,0:T(4,128)(2,1)S(1)} all-reduce(f32[256,4,1536]{2,1,0:T(4,128)} %copy.42), channel_id=2, replica_groups=mesh['pipe'=4,'seq'=32,'batch'=2] {'seq'}, use_global_device_ids=true, to_apply=%region_0.0.clone | all-reduce | flops 1572864 | bytes 9437184
  206.1 8.1 slice.137
  214.3 1057.5 %while.17 = (s32[]{:T(128)}, bf16[16,1536]{1,0:T(8,128)(2,1)S(1)}, f32[16,64]{1,0:T(8,128)S(1)}, s32[]{:T(128)}, pred[]{:T(512)}, /*index=5*/bf16[64,1536]{1,0:T...) while((s32[]{:T(128)}, bf16[16,1536]{1,0:T(8,128)(2,1)S(1)}, ...), condition=%wide.region_10.11_spmd, body=%wide.region_1.10_spmd.sunk | while | flops 464863840 | bytes 43831728 | solution.py:188
  242.1 8.1 all-to-all-start.1
  266.6 8.9 all-to-all-done.2
  284.5 9.3 all-to-all-done.3
  355.0 8.9 all-to-all-done.2
  372.9 9.3 all-to-all-done.3
  418.1 8.1 all-to-all-start.1
  442.5 8.9 all-to-all-done.2
  460.4 9.3 all-to-all-done.3
  531.0 8.9 all-to-all-done.2
  548.9 9.3 all-to-all-done.3
  594.3 8.1 all-to-all-start.1
  618.7 8.9 all-to-all-done.2
  636.6 9.3 all-to-all-done.3
  706.8 8.9 all-to-all-done.2
  724.8 9.6 all-to-all-done.3
  770.3 8.1 all-to-all-start.1
  794.7 8.9 all-to-all-done.2
  812.7 9.3 all-to-all-done.3
  883.0 8.9 all-to-all-done.2
  900.9 9.3 all-to-all-done.3
  946.3 8.1 all-to-all-start.1
  971.2 8.9 all-to-all-done.2
  989.2 9.3 all-to-all-done.3
  1059.4 9.0 all-to-all-done.2
  1077.5 9.3 all-to-all-done.3
  1147.1 8.9 all-to-all-done.2
  1165.1 9.3 all-to-all-done.3
  1235.4 8.9 all-to-all-done.2
  1253.4 9.3 all-to-all-done.3
  (1001 shorter events, 795.0 us)
Async XLA Ops:
  6.5 199.5 %all-gather.6.cloned.1.call-start = ((), (), s32[]{:S(2)}) async-start(), calls=%async_computation.5 | async-start | bytes 21233664 | tf_op jit(solution)/shard_map/all_gather | solution.py:56
  7.3 207.0 %all-gather.4.cloned.1.call-start = ((), (), s32[]{:S(2)}) async-start(), calls=%async_computation.4 | async-start | bytes 3538944 | tf_op jit(solution)/shard_map/all_gather | solution.py:58
  8.0 206.2 %all-gather.8.cloned.1.call-start = ((), (), s32[]{:S(2)}) async-start(), calls=%async_computation.6 | async-start | bytes 7077888 | tf_op jit(solution)/shard_map/all_gather | solution.py:57
  227.7 14.4 %all-to-all-start = ((bf16[32,2,384]{2,1,0:T(2,128)(2,1)}), bf16[32,2,384]{2,1,0:T(2,128)(2,1)S(1)}, u32[]{:S(2)}, u32[]{:S(2)}) async-start(bf16[32,2,384]{2,1,0:T(2,128)(2,1)} %reshape.315), calls=%async_computation | async-start | bytes 98304 | tf_op jit(solution)/shard_map/while/body/eval_jaxpr/all_to_all | solution.py:142
  242.1 18.8 %all-to-all-start.1 = ((bf16[32,2,1152]{2,1,0:T(2,128)(2,1)}), bf16[32,2,1152]{2,1,0:T(2,128)(2,1)S(1)}, u32[]{:S(2)}, u32[]{:S(2)}) async-start(bf16[32,2,1152]{2,1,0:T(2,128)(2,1)} %reshape.319), calls=%async_computation.1 | async-start | bytes 294912 | tf_op jit(solution)/shard_map/while/body/eval_jaxpr/all_to_all | solution.py:143
  260.9 14.6 %all-to-all-start.2 = ((bf16[32,2,1152]{2,1,0:T(2,128)(2,1)}), bf16[32,2,1152]{2,1,0:T(2,128)(2,1)S(1)}, u32[]{:S(2)}, u32[]{:S(2)}) async-start(bf16[32,2,1152]{2,1,0:T(2,128)(2,1)} %reshape.323), calls=%async_computation.2 | async-start | bytes 294912 | tf_op jit(solution)/shard_map/while/body/eval_jaxpr/all_to_all | solution.py:144
  280.1 13.8 %all-to-all-start.3 = ((bf16[32,2,384]{2,1,0:T(2,128)(2,1)}), bf16[32,2,384]{2,1,0:T(2,128)(2,1)S(1)}, u32[]{:S(2)}, u32[]{:S(2)}) async-start(bf16[32,2,384]{2,1,0:T(2,128)(2,1)} %reshape.326), calls=%async_computation.3 | async-start | bytes 98304 | tf_op jit(solution)/shard_map/while/body/eval_jaxpr/all_to_all | solution.py:164
  330.6 18.7 %all-to-all-start.1 = ((bf16[32,2,1152]{2,1,0:T(2,128)(2,1)}), bf16[32,2,1152]{2,1,0:T(2,128)(2,1)S(1)}, u32[]{:S(2)}, u32[]{:S(2)}) async-start(bf16[32,2,1152]{2,1,0:T(2,128)(2,1)} %reshape.319), calls=%async_computation.1 | async-start | bytes 294912 | tf_op jit(solution)/shard_map/while/body/eval_jaxpr/all_to_all | solution.py:143
  349.3 14.6 %all-to-all-start.2 = ((bf16[32,2,1152]{2,1,0:T(2,128)(2,1)}), bf16[32,2,1152]{2,1,0:T(2,128)(2,1)S(1)}, u32[]{:S(2)}, u32[]{:S(2)}) async-start(bf16[32,2,1152]{2,1,0:T(2,128)(2,1)} %reshape.323), calls=%async_computation.2 | async-start | bytes 294912 | tf_op jit(solution)/shard_map/while/body/eval_jaxpr/all_to_all | solution.py:144
  418.1 18.7 %all-to-all-start.1 = ((bf16[32,2,1152]{2,1,0:T(2,128)(2,1)}), bf16[32,2,1152]{2,1,0:T(2,128)(2,1)S(1)}, u32[]{:S(2)}, u32[]{:S(2)}) async-start(bf16[32,2,1152]{2,1,0:T(2,128)(2,1)} %reshape.319), calls=%async_computation.1 | async-start | bytes 294912 | tf_op jit(solution)/shard_map/while/body/eval_jaxpr/all_to_all | solution.py:143
  436.8 14.6 %all-to-all-start.2 = ((bf16[32,2,1152]{2,1,0:T(2,128)(2,1)}), bf16[32,2,1152]{2,1,0:T(2,128)(2,1)S(1)}, u32[]{:S(2)}, u32[]{:S(2)}) async-start(bf16[32,2,1152]{2,1,0:T(2,128)(2,1)} %reshape.323), calls=%async_computation.2 | async-start | bytes 294912 | tf_op jit(solution)/shard_map/while/body/eval_jaxpr/all_to_all | solution.py:144
  506.5 18.8 %all-to-all-start.1 = ((bf16[32,2,1152]{2,1,0:T(2,128)(2,1)}), bf16[32,2,1152]{2,1,0:T(2,128)(2,1)S(1)}, u32[]{:S(2)}, u32[]{:S(2)}) async-start(bf16[32,2,1152]{2,1,0:T(2,128)(2,1)} %reshape.319), calls=%async_computation.1 | async-start | bytes 294912 | tf_op jit(solution)/shard_map/while/body/eval_jaxpr/all_to_all | solution.py:143
  525.3 14.6 %all-to-all-start.2 = ((bf16[32,2,1152]{2,1,0:T(2,128)(2,1)}), bf16[32,2,1152]{2,1,0:T(2,128)(2,1)S(1)}, u32[]{:S(2)}, u32[]{:S(2)}) async-start(bf16[32,2,1152]{2,1,0:T(2,128)(2,1)} %reshape.323), calls=%async_computation.2 | async-start | bytes 294912 | tf_op jit(solution)/shard_map/while/body/eval_jaxpr/all_to_all | solution.py:144
  594.3 18.8 %all-to-all-start.1 = ((bf16[32,2,1152]{2,1,0:T(2,128)(2,1)}), bf16[32,2,1152]{2,1,0:T(2,128)(2,1)S(1)}, u32[]{:S(2)}, u32[]{:S(2)}) async-start(bf16[32,2,1152]{2,1,0:T(2,128)(2,1)} %reshape.319), calls=%async_computation.1 | async-start | bytes 294912 | tf_op jit(solution)/shard_map/while/body/eval_jaxpr/all_to_all | solution.py:143
  613.0 14.6 %all-to-all-start.2 = ((bf16[32,2,1152]{2,1,0:T(2,128)(2,1)}), bf16[32,2,1152]{2,1,0:T(2,128)(2,1)S(1)}, u32[]{:S(2)}, u32[]{:S(2)}) async-start(bf16[32,2,1152]{2,1,0:T(2,128)(2,1)} %reshape.323), calls=%async_computation.2 | async-start | bytes 294912 | tf_op jit(solution)/shard_map/while/body/eval_jaxpr/all_to_all | solution.py:144
  668.6 13.9 %all-to-all-start = ((bf16[32,2,384]{2,1,0:T(2,128)(2,1)}), bf16[32,2,384]{2,1,0:T(2,128)(2,1)S(1)}, u32[]{:S(2)}, u32[]{:S(2)}) async-start(bf16[32,2,384]{2,1,0:T(2,128)(2,1)} %reshape.315), calls=%async_computation | async-start | bytes 98304 | tf_op jit(solution)/shard_map/while/body/eval_jaxpr/all_to_all | solution.py:142
  682.5 18.6 %all-to-all-start.1 = ((bf16[32,2,1152]{2,1,0:T(2,128)(2,1)}), bf16[32,2,1152]{2,1,0:T(2,128)(2,1)S(1)}, u32[]{:S(2)}, u32[]{:S(2)}) async-start(bf16[32,2,1152]{2,1,0:T(2,128)(2,1)} %reshape.319), calls=%async_computation.1 | async-start | bytes 294912 | tf_op jit(solution)/shard_map/while/body/eval_jaxpr/all_to_all | solution.py:143
  701.1 14.6 %all-to-all-start.2 = ((bf16[32,2,1152]{2,1,0:T(2,128)(2,1)}), bf16[32,2,1152]{2,1,0:T(2,128)(2,1)S(1)}, u32[]{:S(2)}, u32[]{:S(2)}) async-start(bf16[32,2,1152]{2,1,0:T(2,128)(2,1)} %reshape.323), calls=%async_computation.2 | async-start | bytes 294912 | tf_op jit(solution)/shard_map/while/body/eval_jaxpr/all_to_all | solution.py:144
  720.3 14.0 %all-to-all-start.3 = ((bf16[32,2,384]{2,1,0:T(2,128)(2,1)}), bf16[32,2,384]{2,1,0:T(2,128)(2,1)S(1)}, u32[]{:S(2)}, u32[]{:S(2)}) async-start(bf16[32,2,384]{2,1,0:T(2,128)(2,1)} %reshape.326), calls=%async_computation.3 | async-start | bytes 98304 | tf_op jit(solution)/shard_map/while/body/eval_jaxpr/all_to_all | solution.py:164
  770.3 18.8 %all-to-all-start.1 = ((bf16[32,2,1152]{2,1,0:T(2,128)(2,1)}), bf16[32,2,1152]{2,1,0:T(2,128)(2,1)S(1)}, u32[]{:S(2)}, u32[]{:S(2)}) async-start(bf16[32,2,1152]{2,1,0:T(2,128)(2,1)} %reshape.319), calls=%async_computation.1 | async-start | bytes 294912 | tf_op jit(solution)/shard_map/while/body/eval_jaxpr/all_to_all | solution.py:143
  789.1 14.6 %all-to-all-start.2 = ((bf16[32,2,1152]{2,1,0:T(2,128)(2,1)}), bf16[32,2,1152]{2,1,0:T(2,128)(2,1)S(1)}, u32[]{:S(2)}, u32[]{:S(2)}) async-start(bf16[32,2,1152]{2,1,0:T(2,128)(2,1)} %reshape.323), calls=%async_computation.2 | async-start | bytes 294912 | tf_op jit(solution)/shard_map/while/body/eval_jaxpr/all_to_all | solution.py:144
  858.6 18.8 %all-to-all-start.1 = ((bf16[32,2,1152]{2,1,0:T(2,128)(2,1)}), bf16[32,2,1152]{2,1,0:T(2,128)(2,1)S(1)}, u32[]{:S(2)}, u32[]{:S(2)}) async-start(bf16[32,2,1152]{2,1,0:T(2,128)(2,1)} %reshape.319), calls=%async_computation.1 | async-start | bytes 294912 | tf_op jit(solution)/shard_map/while/body/eval_jaxpr/all_to_all | solution.py:143
  877.3 14.6 %all-to-all-start.2 = ((bf16[32,2,1152]{2,1,0:T(2,128)(2,1)}), bf16[32,2,1152]{2,1,0:T(2,128)(2,1)S(1)}, u32[]{:S(2)}, u32[]{:S(2)}) async-start(bf16[32,2,1152]{2,1,0:T(2,128)(2,1)} %reshape.323), calls=%async_computation.2 | async-start | bytes 294912 | tf_op jit(solution)/shard_map/while/body/eval_jaxpr/all_to_all | solution.py:144
  896.5 13.8 %all-to-all-start.3 = ((bf16[32,2,384]{2,1,0:T(2,128)(2,1)}), bf16[32,2,384]{2,1,0:T(2,128)(2,1)S(1)}, u32[]{:S(2)}, u32[]{:S(2)}) async-start(bf16[32,2,384]{2,1,0:T(2,128)(2,1)} %reshape.326), calls=%async_computation.3 | async-start | bytes 98304 | tf_op jit(solution)/shard_map/while/body/eval_jaxpr/all_to_all | solution.py:164
  946.3 19.3 %all-to-all-start.1 = ((bf16[32,2,1152]{2,1,0:T(2,128)(2,1)}), bf16[32,2,1152]{2,1,0:T(2,128)(2,1)S(1)}, u32[]{:S(2)}, u32[]{:S(2)}) async-start(bf16[32,2,1152]{2,1,0:T(2,128)(2,1)} %reshape.319), calls=%async_computation.1 | async-start | bytes 294912 | tf_op jit(solution)/shard_map/while/body/eval_jaxpr/all_to_all | solution.py:143
  965.6 14.6 %all-to-all-start.2 = ((bf16[32,2,1152]{2,1,0:T(2,128)(2,1)}), bf16[32,2,1152]{2,1,0:T(2,128)(2,1)S(1)}, u32[]{:S(2)}, u32[]{:S(2)}) async-start(bf16[32,2,1152]{2,1,0:T(2,128)(2,1)} %reshape.323), calls=%async_computation.2 | async-start | bytes 294912 | tf_op jit(solution)/shard_map/while/body/eval_jaxpr/all_to_all | solution.py:144
  1035.0 18.8 %all-to-all-start.1 = ((bf16[32,2,1152]{2,1,0:T(2,128)(2,1)}), bf16[32,2,1152]{2,1,0:T(2,128)(2,1)S(1)}, u32[]{:S(2)}, u32[]{:S(2)}) async-start(bf16[32,2,1152]{2,1,0:T(2,128)(2,1)} %reshape.319), calls=%async_computation.1 | async-start | bytes 294912 | tf_op jit(solution)/shard_map/while/body/eval_jaxpr/all_to_all | solution.py:143
  1053.8 14.6 %all-to-all-start.2 = ((bf16[32,2,1152]{2,1,0:T(2,128)(2,1)}), bf16[32,2,1152]{2,1,0:T(2,128)(2,1)S(1)}, u32[]{:S(2)}, u32[]{:S(2)}) async-start(bf16[32,2,1152]{2,1,0:T(2,128)(2,1)} %reshape.323), calls=%async_computation.2 | async-start | bytes 294912 | tf_op jit(solution)/shard_map/while/body/eval_jaxpr/all_to_all | solution.py:144
  1122.7 18.8 %all-to-all-start.1 = ((bf16[32,2,1152]{2,1,0:T(2,128)(2,1)}), bf16[32,2,1152]{2,1,0:T(2,128)(2,1)S(1)}, u32[]{:S(2)}, u32[]{:S(2)}) async-start(bf16[32,2,1152]{2,1,0:T(2,128)(2,1)} %reshape.319), calls=%async_computation.1 | async-start | bytes 294912 | tf_op jit(solution)/shard_map/while/body/eval_jaxpr/all_to_all | solution.py:143
  1141.5 14.6 %all-to-all-start.2 = ((bf16[32,2,1152]{2,1,0:T(2,128)(2,1)}), bf16[32,2,1152]{2,1,0:T(2,128)(2,1)S(1)}, u32[]{:S(2)}, u32[]{:S(2)}) async-start(bf16[32,2,1152]{2,1,0:T(2,128)(2,1)} %reshape.323), calls=%async_computation.2 | async-start | bytes 294912 | tf_op jit(solution)/shard_map/while/body/eval_jaxpr/all_to_all | solution.py:144
  1211.0 18.8 %all-to-all-start.1 = ((bf16[32,2,1152]{2,1,0:T(2,128)(2,1)}), bf16[32,2,1152]{2,1,0:T(2,128)(2,1)S(1)}, u32[]{:S(2)}, u32[]{:S(2)}) async-start(bf16[32,2,1152]{2,1,0:T(2,128)(2,1)} %reshape.319), calls=%async_computation.1 | async-start | bytes 294912 | tf_op jit(solution)/shard_map/while/body/eval_jaxpr/all_to_all | solution.py:143
  1229.8 14.6 %all-to-all-start.2 = ((bf16[32,2,1152]{2,1,0:T(2,128)(2,1)}), bf16[32,2,1152]{2,1,0:T(2,128)(2,1)S(1)}, u32[]{:S(2)}, u32[]{:S(2)}) async-start(bf16[32,2,1152]{2,1,0:T(2,128)(2,1)} %reshape.323), calls=%async_computation.2 | async-start | bytes 294912 | tf_op jit(solution)/shard_map/while/body/eval_jaxpr/all_to_all | solution.py:144
  (52 other events, 604.6 us)
Sparse Core Ops, SparseCore 0:
  9.2 34.7 all-gather.5
  45.7 17.5 all-gather.3
  65.1 21.0 all-gather.7
where the time goes:
time: 1280 us
  waiting for transfers between devices  356 us (28%)
  starting transfers between devices  273 us (21%)
  matrix products  225 us (18%)
  blocking collectives  184 us (14%)
  local copies, waits for them, and re-layouts  112 us (9%)
  other arithmetic  97.6 us (8%)
  loops' own time  18.2 us (1%)
  between operations  13.9 us (1%)
    unnamed x1, blocking collectives  184 us
    all_to_all x12, waiting for transfers between devices, one_turn(): lax.all_to_all(attended.reshape(unit_here, seq_count * query_rows * head_...  112 us
    all_to_all x12, waiting for transfers between devices, one_turn(): lax.all_to_all(key_units(joined_values), 'seq', split_axis=0, concat_axis...  107 us
    all_to_all x12, starting transfers between devices, one_turn(): lax.all_to_all(key_units(joined_keys), 'seq', split_axis=0, concat_axis=1...  97.4 us
    all_to_all x12, waiting for transfers between devices, one_turn(): lax.all_to_all(key_units(joined_keys), 'seq', split_axis=0, concat_axis=1...  89 us
    dot_general x12, matrix products, one_turn(): jnp.dot(normed, attn_weight, preferred_element_type=jnp.float32)  84.3 us
    dot_general x12, matrix products, one_turn(): jnp.dot(context_rows, text_scale_weight, preferred_element_type=jnp.float32)  60.1 us
    all_to_all x12, starting transfers between devices, one_turn(): lax.all_to_all(queries, 'seq', split_axis=0, concat_axis=1, tiled=True)  46.7 us
  transfers between devices with their start and end apart: 75, of which 60 were waited for; matrix products, arithmetic and copies ran while one was open for 14% of the time, Pallas kernels for 0%

commit v1 on v0

v1 whole, which is shorter than its diff:
```python
import functools
import math

import jax
import jax.numpy as jnp
from jax import lax
from jax.experimental import pallas as pl
from jax.experimental.pallas import tpu as pltpu
from jax.sharding import Mesh, PartitionSpec as P

HEADS = 16
HEAD = 96
STEPS = 2
BLOCKS = 4
X, Z, Y, C = 4, 8, 4, 2
AXES = ("x", "z", "y", "c")
BF = jnp.bfloat16
F32 = jnp.float32
VMEM = 56 * 1024 * 1024

epsilon = 1e-06


def layer_norm(hidden):
    values = hidden.astype(F32)
    center = values - jnp.mean(values, axis=-1, keepdims=True)
    spread = jnp.mean(center * center, axis=-1, keepdims=True)
    return center * lax.rsqrt(spread + epsilon)


def time_features(noise_level, feature_count):
    half_count = feature_count // 2
    wave_frequency = jnp.exp(
        -math.log(10000.0) * jnp.arange(half_count, dtype=F32) / half_count
    )
    angles = noise_level * wave_frequency
    return jnp.concatenate([jnp.cos(angles), jnp.sin(angles)]).astype(BF)


def flat(x, z, y, c):
    return ((x * Z + z) * Y + y) * C + c


def move(value, pairs):
    return lax.ppermute(value, AXES, [(flat(*a), flat(*b)) for a, b in pairs])


def homes():
    return [(z // 2, z, z % 2) for z in range(Z)]


def product_kernel(core_ref, rows_ref, shift_ref, scale_ref, own_ref, other_ref, out_ref, normed, *, norm):
    half = own_ref.shape[0]
    total = rows_ref.shape[0]
    step = min(total, 128)

    @pl.when(pl.program_id(0) == 0)
    def _():
        def body(i, carry):
            rows = pl.ds(pl.multiple_of(i * step, step), step)
            values = rows_ref[rows, :].astype(F32)
            if norm:
                center = values - jnp.mean(values, axis=-1, keepdims=True)
                spread = jnp.mean(center * center, axis=-1, keepdims=True)
                values = center * lax.rsqrt(spread + epsilon)
                values = values * (1.0 + scale_ref[...]) + shift_ref[...]
            normed[rows, :] = values.astype(BF)
            return carry

        lax.fori_loop(0, total // step, body, 0)

    core = core_ref[0]
    mine = pl.ds(pl.multiple_of(core * half, 128), half)
    theirs = pl.ds(pl.multiple_of((1 - core) * half, 128), half)
    out_ref[...] = (
        jnp.dot(normed[:, mine], own_ref[...], preferred_element_type=F32)
        + jnp.dot(normed[:, theirs], other_ref[...], preferred_element_type=F32)
    ).astype(BF)


def product(core, rows, shift, scale, own, other, first, columns, norm, block=512):
    count, width = rows.shape
    half = own.shape[0]
    start = first // block
    return pl.pallas_call(
        functools.partial(product_kernel, norm=norm),
        grid=(columns // block,),
        in_specs=[
            pl.BlockSpec(memory_space=pltpu.SMEM),
            pl.BlockSpec((count, width), lambda i: (0, 0)),
            pl.BlockSpec((1, width), lambda i: (0, 0)),
            pl.BlockSpec((1, width), lambda i: (0, 0)),
            pl.BlockSpec((half, block), lambda i: (0, i + start)),
            pl.BlockSpec((half, block), lambda i: (0, i + start)),
        ],
        out_specs=pl.BlockSpec((count, block), lambda i: (0, i)),
        out_shape=jax.ShapeDtypeStruct((count, columns), BF),
        scratch_shapes=[pltpu.VMEM((count, width), BF)],
        compiler_params=pltpu.CompilerParams(vmem_limit_bytes=VMEM),
        name="product",
    )(core, rows, shift, scale, own, other)


def attention_kernel(
    core_ref, q_ref, k_ref, v_ref, kt_ref, vt_ref, bias_ref, hidden_ref, gate_ref, own_ref, other_ref, out_ref, attended
):
    rows = q_ref.shape[0]
    half = own_ref.shape[0]
    factor = math.log2(math.e) / math.sqrt(HEAD)
    lanes = lax.broadcasted_iota(jnp.int32, (1, 128), 1)
    wide = lax.broadcasted_iota(jnp.int32, (1, 256), 1)
    bias = bias_ref[...]
    contract = (((1,), (1,)), ((), ()))

    def group(g, carry):
        base = pl.multiple_of(g * 4 * HEAD, 128)
        outs = []
        for h in range(4):
            low, high = h * HEAD, (h + 1) * HEAD
            start, stop = low // 128 * 128, -(-high // 128) * 128
            width = stop - start
            window = pl.ds(pl.multiple_of(base + start, 128), width)
            index = lanes if width == 128 else wide
            mask = ((index >= low - start) & (index < high - start)).astype(F32).astype(BF)
            q = q_ref[:, window] * mask
            image = lax.dot_general(q, k_ref[:, window], contract, preferred_element_type=F32)
            text = lax.dot_general(q, kt_ref[:, window], contract, preferred_element_type=F32) + bias
            top = jnp.maximum(
                jnp.max(image, axis=-1, keepdims=True), jnp.max(text, axis=-1, keepdims=True)
            )
            image = jnp.exp2((image - top) * factor)
            text = jnp.exp2((text - top) * factor)
            total = jnp.sum(image, axis=-1, keepdims=True) + jnp.sum(text, axis=-1, keepdims=True)
            value = jnp.dot(image.astype(BF), v_ref[:, window], preferred_element_type=F32) + jnp.dot(
                text.astype(BF), vt_ref[:, window], preferred_element_type=F32
            )
            outs.append(value * (1.0 / total))
        tiles = (
            jnp.where(lanes < 96, outs[0], outs[1][:, :128]),
            jnp.where(lanes < 64, outs[1][:, 128:], outs[2][:, :128]),
            jnp.where(lanes < 32, outs[2][:, 128:], outs[3]),
        )
        for j, tile in enumerate(tiles):
            attended[:, pl.ds(pl.multiple_of(base + j * 128, 128), 128)] = tile.astype(BF)
        return carry

    lax.fori_loop(0, HEADS // 4, group, 0)
    core = core_ref[0]
    mine = pl.ds(pl.multiple_of(core * half, 128), half)
    theirs = pl.ds(pl.multiple_of((1 - core) * half, 128), half)
    update = jnp.dot(attended[:, mine], own_ref[...], preferred_element_type=F32) + jnp.dot(
        attended[:, theirs], other_ref[...], preferred_element_type=F32
    )
    out_ref[...] = (hidden_ref[...].astype(F32) + gate_ref[...] * update).astype(BF)


def attention(core, qkv, text, bias, hidden, gate, own, other, block=256):
    count, width = hidden.shape
    text_count = text.shape[0]
    half = own.shape[0]
    return pl.pallas_call(
        attention_kernel,
        grid=(count // block,),
        in_specs=[
            pl.BlockSpec(memory_space=pltpu.SMEM),
            pl.BlockSpec((block, width), lambda i: (i, 0)),
            pl.BlockSpec((count, width), lambda i: (0, 1)),
            pl.BlockSpec((count, width), lambda i: (0, 2)),
            pl.BlockSpec((text_count, width), lambda i: (0, 0)),
            pl.BlockSpec((text_count, width), lambda i: (0, 1)),
            pl.BlockSpec((1, text_count), lambda i: (0, 0)),
            pl.BlockSpec((block, width), lambda i: (i, 0)),
            pl.BlockSpec((1, width), lambda i: (0, 0)),
            pl.BlockSpec((half, width), lambda i: (0, 0)),
            pl.BlockSpec((half, width), lambda i: (0, 0)),
        ],
        out_specs=pl.BlockSpec((block, width), lambda i: (i, 0)),
        out_shape=jax.ShapeDtypeStruct((count, width), BF),
        scratch_shapes=[pltpu.VMEM((block, width), BF)],
        compiler_params=pltpu.CompilerParams(vmem_limit_bytes=VMEM),
        name="attention",
    )(core, qkv, qkv, qkv, text, text, bias, hidden, gate, own, other)


def on_device(
    latent_noise,
    text_rows,
    text_lengths,
    plan,
    context_weight,
    w_embed,
    w_attention,
    w_project,
    w_modulate,
    w_final,
):
    x, z, y, c = (lax.axis_index(name) for name in AXES)
    width = w_embed.shape[1]
    latent_width = latent_noise.shape[3]
    patches = latent_noise.shape[2] * Z * Y
    text_total = text_rows.shape[2]
    core = jnp.reshape(c, (1,)).astype(jnp.int32)
    image = z // 2

    across = [((a, b, 0, 1 - b % 2), (a, b, 0, b % 2)) for a in range(X) for b in range(Z)]
    attn_own, proj_own, mod_own = w_attention[0], w_project[0], w_modulate[0]
    levels = plan.astype(F32)
    features = jnp.stack([time_features(levels[k], 2 * mod_own.shape[0]) for k in range(STEPS)])
    features = lax.dynamic_slice_in_dim(features, c * mod_own.shape[0], mod_own.shape[0], 1)
    modulation = jnp.dot(features, mod_own, preferred_element_type=F32)

    text = lax.dynamic_index_in_dim(text_rows[:, 0], x, 0, keepdims=False)
    partial = jnp.dot(text, context_weight, preferred_element_type=F32).astype(BF)
    quarter = text_total // Y
    parts = lax.all_to_all(
        partial.reshape(Y, quarter, width), "y", split_axis=0, concat_axis=0, tiled=True
    )
    summed = jnp.sum(parts.astype(F32), axis=0)
    rows_here = latent_noise.shape[2]
    latent = latent_noise[0, 0].reshape(-1)
    high = latent.astype(BF)
    low = (latent - high.astype(F32)).astype(BF)
    carried = -(-latent.size // width) * width
    pad = lambda value: jnp.pad(value, (0, carried - value.size)).reshape(-1, width)
    extra = jnp.concatenate([pad(high), pad(low)], 0)
    extra_rows = extra.shape[0]
    message = jnp.concatenate([summed.astype(BF), extra], 0)
    total = summed
    here = 2 * x + c
    pieces = jnp.zeros((Z, extra_rows, width), BF)
    pieces = lax.dynamic_update_index_in_dim(pieces, extra, here % Z, 0)
    for k in range(1, Z):
        got = move(
            message,
            [
                ((a, (2 * a + d + k) % Z, b, d), (a, 2 * a + d, b, d))
                for a in range(X)
                for b in range(Y)
                for d in range(C)
            ],
        )
        total = total + got[:quarter].astype(F32)
        pieces = lax.dynamic_update_index_in_dim(pieces, got[quarter:], (here + k) % Z, 0)
    message = jnp.concatenate([total.astype(BF), pieces.reshape(Z * extra_rows, width)], 0)
    shared = jnp.where(x == image, message, jnp.zeros_like(message))
    for k in range(1, X):
        shared = shared + move(
            message,
            [((m, b, a, d), ((m + k) % X, b, a, d)) for m, b, d in homes() for a in range(Y)],
        )
    gathered = [shared]
    for k in range(1, Y):
        gathered.append(move(shared, [((a, b, k, d), (a, b, 0, d)) for a in range(X) for _, b, d in homes()]))
    context = jnp.concatenate([part[:quarter] for part in gathered], 0)

    def latent_of(part):
        flat_rows = part[quarter:].reshape(Z, 2, carried)[:, :, : rows_here * latent_width]
        return flat_rows.reshape(Z, 2, rows_here, latent_width)

    latents = jnp.stack([latent_of(part) for part in gathered], 1)
    latent_high = latents[:, :, 0].reshape(patches, latent_width)
    latent_low = latents[:, :, 1].reshape(patches, latent_width)
    latent = latent_high.astype(F32) + latent_low.astype(F32)

    attn_other = move(attn_own, across)
    proj_other = move(proj_own, across)
    modulation = modulation + move(modulation, across)

    length = jnp.sum(jnp.where(jnp.arange(X) == image, text_lengths[:, 0], 0))
    bias = jnp.where(jnp.arange(text_total) < length, 0.0, -1e30).astype(F32)[None, :]
    nothing = jnp.zeros((1, width), F32)
    pairs_text = product(
        core, context, nothing, nothing, attn_own, attn_other, width, 2 * width, False
    )

    hidden = jnp.dot(latent_high, w_embed, preferred_element_type=F32).astype(BF)
    for turn in range(STEPS * BLOCKS):
        step, block = divmod(turn, BLOCKS)
        shift = modulation[step : step + 1, :width]
        scale = modulation[step : step + 1, width : 2 * width]
        gate = modulation[step : step + 1, 2 * width :]
        qkv = product(core, hidden, shift, scale, attn_own, attn_other, 0, 3 * width, True)
        hidden = attention(core, qkv, pairs_text, bias, hidden, gate, proj_own, proj_other)
        if block < BLOCKS - 1:
            hidden = move(
                hidden, [((block, b, 0, d), (block + 1, b, 0, d)) for _, b, d in homes()]
            )
        else:
            velocity = jnp.dot(
                layer_norm(hidden).astype(BF), w_final, preferred_element_type=F32
            )
            latent = latent + (levels[step + 1] - levels[step]) / 1000.0 * velocity
            if step < STEPS - 1:
                first = move(
                    latent.astype(BF), [((block, b, 0, d), (0, b, 0, d)) for _, b, d in homes()]
                )
                hidden = jnp.dot(first, w_embed, preferred_element_type=F32).astype(BF)

    last = BLOCKS - 1
    moved = move(latent, [((last, b, 0, d), (m, b, 0, d)) for m, b, d in homes() if m != last])
    latent = jnp.where(x == last, latent, moved)
    spread = lax.all_to_all(
        latent.reshape(Z * Y, rows_here, latent_width),
        ("z", "y"),
        split_axis=0,
        concat_axis=0,
        tiled=True,
    )
    mine = lax.dynamic_index_in_dim(spread, here * Y, 0, keepdims=False)
    return mine.reshape(latent_noise.shape)


def solution(mesh):
    inner = Mesh(mesh.devices.reshape(X, Z, Y, C), AXES)
    seq = ("z", "y")
    placed = (
        P("x", "c", seq, None),
        P(None, "c", None, seq),
        P(None, "c"),
        P(),
        P(seq, None),
        P(),
        P("x", "c", None),
        P("x", "c", None),
        P("x", "c", None),
        P(),
    )
    return jax.shard_map(
        on_device,
        mesh=inner,
        in_specs=placed,
        out_specs=P("x", "c", seq, None),
        check_vma=False,
    )
```

time: 1280 us -> 587 us (0.46)
  Pallas kernels: 0 us -> 295 us
  matrix products: 225 us -> 8.33 us
  starting transfers between devices: 273 us -> 68.3 us
  waiting for transfers between devices: 356 us -> 164 us
  blocking collectives: 184 us -> 0 us
  local copies, waits for them, and re-layouts: 112 us -> 21.9 us
  other arithmetic: 97.6 us -> 13.7 us
  loops' own time: 18.2 us -> 0 us
    all_to_all x48 -> x2, waiting for transfers between devices: 328 us -> 16.9 us  [the longest x1 10.5 us: on_device(): lax.all_to_all(latent.reshape(Z * Y, rows_here, latent_width), ('z', 'y')...]
    pallas_call x0 -> x17, Pallas kernels: none -> 295 us  [the longest x8 163 us: attention(): pl.pallas_call(attention_kernel, grid=(count // block,), in_specs=[pl.Blo...]
    dot_general x97 -> x6, matrix products: 225 us -> 8.33 us  [the longest x1 2.42 us: on_device(): jnp.dot(text, context_weight, preferred_element_type=F32).astype(BF)]
    all_to_all x48 -> x2, starting transfers between devices: 237 us -> 37.9 us  [the longest x1 33.3 us: on_device(): lax.all_to_all(latent.reshape(Z * Y, rows_here, latent_width), ('z', 'y')...]
    unnamed x1 -> x0, blocking collectives: 184 us -> none
    ppermute x24, waiting for transfers between devices: 25.7 us -> 147 us  [move(): return lax.ppermute(value, AXES, [(flat(*a), flat(*b)) for a, b in pairs])]
    all_to_all x72 -> x1, other arithmetic: 68.8 us -> 0.95 us  [on_device(): lax.all_to_all(latent.reshape(Z * Y, rows_here, latent_width), ('z', 'y')...]
    while x109 -> x0, local copies, waits for them, and re-layouts: 41.6 us -> none
  transfers between devices with their start and end apart: 75 -> 26, of which waited for: 60 -> 9; matrix products, arithmetic and copies ran while one was open for 14% -> 3% of each run, Pallas kernels for 0% -> 4%
where the time goes in v1:
time: 587 us; the launch traced here: 576 us
  Pallas kernels  295 us (50%)
  waiting for transfers between devices  164 us (28%)
  starting transfers between devices  68.3 us (12%)
  local copies, waits for them, and re-layouts  21.9 us (4%)
  other arithmetic  13.7 us (2%)
  matrix products  8.33 us (1%)
    pallas_call x8, Pallas kernels, attention(): pl.pallas_call(attention_kernel, grid=(count // block,), in_specs=[pl.Blo...  163 us
    ppermute x24, waiting for transfers between devices, move(): return lax.ppermute(value, AXES, [(flat(*a), flat(*b)) for a, b in pairs])  147 us
    pallas_call x9, Pallas kernels, product(): pl.pallas_call(functools.partial(product_kernel, norm=norm), grid=(column...  132 us
    all_to_all x1, starting transfers between devices, on_device(): lax.all_to_all(latent.reshape(Z * Y, rows_here, latent_width), ('z', 'y')...  33.3 us
    ppermute x24, starting transfers between devices, move(): return lax.ppermute(value, AXES, [(flat(*a), flat(*b)) for a, b in pairs])  30.4 us
    unnamed x55, local copies, waits for them, and re-layouts  13.2 us
  transfers between devices with their start and end apart: 26, of which 9 were waited for; matrix products, arithmetic and copies ran while one was open for 3% of the time, Pallas kernels for 4%

profile of v1, /device:TPU:2, one launch (start us, length us, event | category | flops | bytes accessed | tf_op | source)
XLA Modules:
  0.0 575.6 jit_solution(14801984926169858777)
XLA Ops:
  0.0 2.4 convolution_convert_fusion.2
  2.4 4.6 all-to-all-start
  12.9 6.4 %all-to-all-done = bf16[4,64,1536]{2,1,0:T(8,128)(2,1)S(1)} async-done(((bf16[4,64,1536]{2,1,0:T(8,128)(2,1)}), bf16[4,64,1536]{2,1,0:T(8,128)(2,1)S(1)}, u32[]{:S(2)}, u32[]{:S(2)}) %all-to-all-start) | async-done | bytes 786464 | tf_op jit(solution)/shard_map/all_to_all | solution.py:215
  21.1 6.4 %collective-permute-start.5 = (bf16[66,1536]{1,0:T(8,128)(2,1)S(1)}, bf16[66,1536]{1,0:T(8,128)(2,1)S(1)}, u32[]{:S(2)}, u32[]{:S(2)}) collective-permute-start(bf16[66,1536]{1,0:T(8,128)(2,1)S(1)} %pad_maximum_fusion.2), channel_id=1, source_target_pairs={{48,0},{57,9},{50,2},{59,11},{52,4},{61,13},{54,6},{63,15},{64,80}... | collective-permute-start | bytes 608264 | tf_op jit(solution)/shard_map/ppermute | solution.py:45
  41.2 39.2 %collective-permute-done.7 = bf16[80,1536]{1,0:T(8,128)(2,1)S(1)} collective-permute-done((bf16[80,1536]{1,0:T(8,128)(2,1)S(1)}, bf16[80,1536]{1,0:T(8,128)(2,1)S(1)}, u32[]{:S(2)}, u32[]{:S(2)}) %collective-permute-start.7) | collective-permute-done | bytes 245792 | tf_op jit(solution)/shard_map/ppermute | solution.py:45
  87.7 6.5 %collective-permute-done.12 = bf16[80,1536]{1,0:T(8,128)(2,1)S(1)} collective-permute-done((bf16[80,1536]{1,0:T(8,128)(2,1)S(1)}, bf16[80,1536]{1,0:T(8,128)(2,1)S(1)}, u32[]{:S(2)}, u32[]{:S(2)}) %collective-permute-start.12) | collective-permute-done | bytes 245792 | tf_op jit(solution)/shard_map/ppermute | solution.py:45
  105.2 8.2 %product.10.kt_ref.vt_ref = bf16[256,3072]{1,0:T(8,128)(2,1)} custom-call(s32[1]{0:T(128)} %bitcast.14.core_ref, bf16[256,1536]{1,0:T(8,128)(2,1)} %pad_maximum_fusion.rows_ref, f32[1,1536]{1,0:T(1,128)} %broadcast_in_dim.61.shift_ref.scale_ref, f32[1,1536]{1,0:T(1,128)} %broadcast_in_dim.61.shift_ref.scale_ref, bf16[768,4608]{1,0:T(8,128)(2,1)} %bitcast.80, ...), custom_call_target="tpu_custom_call" | custom-call | tf_op jit(solution)/shard_map/product/pallas_call | solution.py:85
  113.3 15.5 %product.9.q_ref.k_ref.v_ref = bf16[512,4608]{1,0:T(8,128)(2,1)} custom-call(s32[1]{0:T(128)} %bitcast.14.core_ref, bf16[512,1536]{1,0:T(8,128)(2,1)} %convolution_convert_fusion.1.rows_ref.hidden_ref, f32[1,1536]{1,0:T(1,128)} %get-tuple-element.14.shift_ref, f32[1,1536]{1,0:T(1,128)} %get-tuple-element.13.scale_ref, bf16[768,4608]{1,0:T(8,128)(2,1)} %bitcast.81, ...), custom_call_target="tpu_custom_call" | custom-call | tf_op jit(solution)/shard_map/product/pallas_call | solution.py:85
  128.8 20.4 %attention.8 = bf16[512,1536]{1,0:T(8,128)(2,1)} custom-call(s32[1]{0:T(128)} %bitcast.14.core_ref, bf16[512,4608]{1,0:T(8,128)(2,1)} %product.9.q_ref.k_ref.v_ref, bf16[512,4608]{1,0:T(8,128)(2,1)} %product.9.q_ref.k_ref.v_ref, bf16[512,4608]{1,0:T(8,128)(2,1)} %product.9.q_ref.k_ref.v_ref, bf16[256,3072]{1,0:T(8,128)(2,1)} %product.10.kt_ref.vt_ref, ...), custom_call_target="tpu_custom_call" | custom-call | tf_op jit(solution)/shard_map/attention/pallas_call | solution.py:161
  150.5 21.2 %collective-permute-done.16.rows_ref.hidden_ref = bf16[512,1536]{1,0:T(8,128)(2,1)S(1)} collective-permute-done((bf16[512,1536]{1,0:T(8,128)(2,1)}, bf16[512,1536]{1,0:T(8,128)(2,1)S(1)}, u32[]{:S(2)}, u32[]{:S(2)}) %collective-permute-start.16) | collective-permute-done | bytes 1572896 | tf_op jit(solution)/shard_map/ppermute | solution.py:45
  172.9 15.5 %product.11.q_ref.k_ref.v_ref = bf16[512,4608]{1,0:T(8,128)(2,1)} custom-call(s32[1]{0:T(128)} %bitcast.14.core_ref, bf16[512,1536]{1,0:T(8,128)(2,1)} %copy-done.7, f32[1,1536]{1,0:T(1,128)} %get-tuple-element.14.shift_ref, f32[1,1536]{1,0:T(1,128)} %get-tuple-element.13.scale_ref, bf16[768,4608]{1,0:T(8,128)(2,1)} %bitcast.82, ...), custom_call_target="tpu_custom_call" | custom-call | tf_op jit(solution)/shard_map/product/pallas_call | solution.py:85
  188.3 20.4 %attention.9 = bf16[512,1536]{1,0:T(8,128)(2,1)} custom-call(s32[1]{0:T(128)} %bitcast.14.core_ref, bf16[512,4608]{1,0:T(8,128)(2,1)} %product.11.q_ref.k_ref.v_ref, bf16[512,4608]{1,0:T(8,128)(2,1)} %product.11.q_ref.k_ref.v_ref, bf16[512,4608]{1,0:T(8,128)(2,1)} %product.11.q_ref.k_ref.v_ref, bf16[256,3072]{1,0:T(8,128)(2,1)} %product.10.kt_ref.vt_ref, ...), custom_call_target="tpu_custom_call" | custom-call | tf_op jit(solution)/shard_map/attention/pallas_call | solution.py:161
  210.3 18.0 %collective-permute-done.17.rows_ref.hidden_ref = bf16[512,1536]{1,0:T(8,128)(2,1)S(1)} collective-permute-done((bf16[512,1536]{1,0:T(8,128)(2,1)}, bf16[512,1536]{1,0:T(8,128)(2,1)S(1)}, u32[]{:S(2)}, u32[]{:S(2)}) %collective-permute-start.17) | collective-permute-done | bytes 1572896 | tf_op jit(solution)/shard_map/ppermute | solution.py:45
  229.4 15.5 %product.12.q_ref.k_ref.v_ref = bf16[512,4608]{1,0:T(8,128)(2,1)} custom-call(s32[1]{0:T(128)} %bitcast.14.core_ref, bf16[512,1536]{1,0:T(8,128)(2,1)} %copy-done.8, f32[1,1536]{1,0:T(1,128)} %get-tuple-element.14.shift_ref, f32[1,1536]{1,0:T(1,128)} %get-tuple-element.13.scale_ref, bf16[768,4608]{1,0:T(8,128)(2,1)} %bitcast.83, ...), custom_call_target="tpu_custom_call" | custom-call | tf_op jit(solution)/shard_map/product/pallas_call | solution.py:85
  244.9 20.4 %attention.10 = bf16[512,1536]{1,0:T(8,128)(2,1)} custom-call(s32[1]{0:T(128)} %bitcast.14.core_ref, bf16[512,4608]{1,0:T(8,128)(2,1)} %product.12.q_ref.k_ref.v_ref, bf16[512,4608]{1,0:T(8,128)(2,1)} %product.12.q_ref.k_ref.v_ref, bf16[512,4608]{1,0:T(8,128)(2,1)} %product.12.q_ref.k_ref.v_ref, bf16[256,3072]{1,0:T(8,128)(2,1)} %product.10.kt_ref.vt_ref, ...), custom_call_target="tpu_custom_call" | custom-call | tf_op jit(solution)/shard_map/attention/pallas_call | solution.py:161
  268.7 15.5 %product.13.q_ref.k_ref.v_ref = bf16[512,4608]{1,0:T(8,128)(2,1)} custom-call(s32[1]{0:T(128)} %bitcast.14.core_ref, bf16[512,1536]{1,0:T(8,128)(2,1)} %copy-done.6, f32[1,1536]{1,0:T(1,128)} %get-tuple-element.14.shift_ref, f32[1,1536]{1,0:T(1,128)} %get-tuple-element.13.scale_ref, bf16[768,4608]{1,0:T(8,128)(2,1)} %bitcast.84, ...), custom_call_target="tpu_custom_call" | custom-call | tf_op jit(solution)/shard_map/product/pallas_call | solution.py:85
  284.2 20.4 %attention.11 = bf16[512,1536]{1,0:T(8,128)(2,1)} custom-call(s32[1]{0:T(128)} %bitcast.14.core_ref, bf16[512,4608]{1,0:T(8,128)(2,1)} %product.13.q_ref.k_ref.v_ref, bf16[512,4608]{1,0:T(8,128)(2,1)} %product.13.q_ref.k_ref.v_ref, bf16[512,4608]{1,0:T(8,128)(2,1)} %product.13.q_ref.k_ref.v_ref, bf16[256,3072]{1,0:T(8,128)(2,1)} %product.10.kt_ref.vt_ref, ...), custom_call_target="tpu_custom_call" | custom-call | tf_op jit(solution)/shard_map/attention/pallas_call | solution.py:161
  304.6 1.8 convert_reduce_fusion.1
  308.7 1.7 convolution_convert_fusion.rows_ref.hidden_ref
  310.4 15.5 %product.14.q_ref.k_ref.v_ref = bf16[512,4608]{1,0:T(8,128)(2,1)} custom-call(s32[1]{0:T(128)} %bitcast.14.core_ref, bf16[512,1536]{1,0:T(8,128)(2,1)} %convolution_convert_fusion.rows_ref.hidden_ref, f32[1,1536]{1,0:T(1,128)} %get-tuple-element.11.shift_ref, f32[1,1536]{1,0:T(1,128)} %get-tuple-element.10.scale_ref, bf16[768,4608]{1,0:T(8,128)(2,1)} %bitcast.85, ...), custom_call_target="tpu_custom_call" | custom-call | tf_op jit(solution)/shard_map/product/pallas_call | solution.py:85
  325.9 20.4 %attention.12 = bf16[512,1536]{1,0:T(8,128)(2,1)} custom-call(s32[1]{0:T(128)} %bitcast.14.core_ref, bf16[512,4608]{1,0:T(8,128)(2,1)} %product.14.q_ref.k_ref.v_ref, bf16[512,4608]{1,0:T(8,128)(2,1)} %product.14.q_ref.k_ref.v_ref, bf16[512,4608]{1,0:T(8,128)(2,1)} %product.14.q_ref.k_ref.v_ref, bf16[256,3072]{1,0:T(8,128)(2,1)} %product.10.kt_ref.vt_ref, ...), custom_call_target="tpu_custom_call" | custom-call | tf_op jit(solution)/shard_map/attention/pallas_call | solution.py:161
  347.6 43.8 %collective-permute-done.20.rows_ref.hidden_ref = bf16[512,1536]{1,0:T(8,128)(2,1)S(1)} collective-permute-done((bf16[512,1536]{1,0:T(8,128)(2,1)}, bf16[512,1536]{1,0:T(8,128)(2,1)S(1)}, u32[]{:S(2)}, u32[]{:S(2)}) %collective-permute-start.20) | collective-permute-done | bytes 1572896 | tf_op jit(solution)/shard_map/ppermute | solution.py:45
  392.5 15.5 %product.15.q_ref.k_ref.v_ref = bf16[512,4608]{1,0:T(8,128)(2,1)} custom-call(s32[1]{0:T(128)} %bitcast.14.core_ref, bf16[512,1536]{1,0:T(8,128)(2,1)} %copy-done.9, f32[1,1536]{1,0:T(1,128)} %get-tuple-element.11.shift_ref, f32[1,1536]{1,0:T(1,128)} %get-tuple-element.10.scale_ref, bf16[768,4608]{1,0:T(8,128)(2,1)} %bitcast.86, ...), custom_call_target="tpu_custom_call" | custom-call | tf_op jit(solution)/shard_map/product/pallas_call | solution.py:85
  408.0 20.4 %attention.13 = bf16[512,1536]{1,0:T(8,128)(2,1)} custom-call(s32[1]{0:T(128)} %bitcast.14.core_ref, bf16[512,4608]{1,0:T(8,128)(2,1)} %product.15.q_ref.k_ref.v_ref, bf16[512,4608]{1,0:T(8,128)(2,1)} %product.15.q_ref.k_ref.v_ref, bf16[512,4608]{1,0:T(8,128)(2,1)} %product.15.q_ref.k_ref.v_ref, bf16[256,3072]{1,0:T(8,128)(2,1)} %product.10.kt_ref.vt_ref, ...), custom_call_target="tpu_custom_call" | custom-call | tf_op jit(solution)/shard_map/attention/pallas_call | solution.py:161
  429.8 18.1 %collective-permute-done.21.rows_ref.hidden_ref = bf16[512,1536]{1,0:T(8,128)(2,1)S(1)} collective-permute-done((bf16[512,1536]{1,0:T(8,128)(2,1)}, bf16[512,1536]{1,0:T(8,128)(2,1)S(1)}, u32[]{:S(2)}, u32[]{:S(2)}) %collective-permute-start.21) | collective-permute-done | bytes 1572896 | tf_op jit(solution)/shard_map/ppermute | solution.py:45
  449.1 15.5 %product.16.q_ref.k_ref.v_ref = bf16[512,4608]{1,0:T(8,128)(2,1)} custom-call(s32[1]{0:T(128)} %bitcast.14.core_ref, bf16[512,1536]{1,0:T(8,128)(2,1)} %copy-done.10, f32[1,1536]{1,0:T(1,128)} %get-tuple-element.11.shift_ref, f32[1,1536]{1,0:T(1,128)} %get-tuple-element.10.scale_ref, bf16[768,4608]{1,0:T(8,128)(2,1)} %bitcast.87, ...), custom_call_target="tpu_custom_call" | custom-call | tf_op jit(solution)/shard_map/product/pallas_call | solution.py:85
  464.5 20.4 %attention.14 = bf16[512,1536]{1,0:T(8,128)(2,1)} custom-call(s32[1]{0:T(128)} %bitcast.14.core_ref, bf16[512,4608]{1,0:T(8,128)(2,1)} %product.16.q_ref.k_ref.v_ref, bf16[512,4608]{1,0:T(8,128)(2,1)} %product.16.q_ref.k_ref.v_ref, bf16[512,4608]{1,0:T(8,128)(2,1)} %product.16.q_ref.k_ref.v_ref, bf16[256,3072]{1,0:T(8,128)(2,1)} %product.10.kt_ref.vt_ref, ...), custom_call_target="tpu_custom_call" | custom-call | tf_op jit(solution)/shard_map/attention/pallas_call | solution.py:161
  488.4 15.5 %product.17.q_ref.k_ref.v_ref = bf16[512,4608]{1,0:T(8,128)(2,1)} custom-call(s32[1]{0:T(128)} %bitcast.14.core_ref, bf16[512,1536]{1,0:T(8,128)(2,1)} %copy-done.5, f32[1,1536]{1,0:T(1,128)} %get-tuple-element.11.shift_ref, f32[1,1536]{1,0:T(1,128)} %get-tuple-element.10.scale_ref, bf16[768,4608]{1,0:T(8,128)(2,1)} %bitcast.88, ...), custom_call_target="tpu_custom_call" | custom-call | tf_op jit(solution)/shard_map/product/pallas_call | solution.py:85
  503.8 20.4 %attention.15 = bf16[512,1536]{1,0:T(8,128)(2,1)} custom-call(s32[1]{0:T(128)} %bitcast.14.core_ref, bf16[512,4608]{1,0:T(8,128)(2,1)} %product.17.q_ref.k_ref.v_ref, bf16[512,4608]{1,0:T(8,128)(2,1)} %product.17.q_ref.k_ref.v_ref, bf16[512,4608]{1,0:T(8,128)(2,1)} %product.17.q_ref.k_ref.v_ref, bf16[256,3072]{1,0:T(8,128)(2,1)} %product.10.kt_ref.vt_ref, ...), custom_call_target="tpu_custom_call" | custom-call | tf_op jit(solution)/shard_map/attention/pallas_call | solution.py:161
  524.3 1.8 convert_reduce_fusion
  529.2 33.3 %all-to-all-start.1 = ((f32[32,1,1024]{2,1,0:T(1,128)}), f32[32,1,1024]{2,1,0:T(1,128)S(1)}, u32[]{:S(2)}, u32[]{:S(2)}) async-start(f32[32,1,1024]{2,1,0:T(1,128)} %reshape.134), calls=%async_computation.1 | async-start | bytes 262144 | tf_op jit(solution)/shard_map/all_to_all | solution.py:302
  562.5 10.5 %all-to-all-done.1 = f32[32,1,1024]{2,1,0:T(1,128)S(1)} async-done(((f32[32,1,1024]{2,1,0:T(1,128)}), f32[32,1,1024]{2,1,0:T(1,128)S(1)}, u32[]{:S(2)}, u32[]{:S(2)}) %all-to-all-start.1) | async-done | bytes 131104 | tf_op jit(solution)/shard_map/all_to_all | solution.py:302
  (173 shorter events, 60.7 us)
Async XLA Ops:
  0.0 9.0 %copy-start = (bf16[1,128,4608]{2,1,0:T(8,128)(2,1)S(1)}, bf16[1,128,4608]{2,1,0:T(8,128)(2,1)}, u32[]{:S(2)}) copy-start(bf16[1,128,4608]{2,1,0:T(8,128)(2,1)} %param.18) | copy-start | bytes 3538948
  0.0 7.0 %copy-start.23 = (s32[3]{0:T(128)S(1)}, s32[3]{0:T(128)}, u32[]{:S(2)}) copy-start(s32[3]{0:T(128)} %param.13) | copy-start | bytes 40
  2.4 10.3 %copy-start.21 = (f32[1,1,16,64]{3,2,1,0:T(8,128)S(1)}, f32[1,1,16,64]{3,2,1,0:T(8,128)}, u32[]{:S(2)}) copy-start(f32[1,1,16,64]{3,2,1,0:T(8,128)} %param.10) | copy-start | bytes 12292
  2.4 16.9 %all-to-all-start = ((bf16[4,64,1536]{2,1,0:T(8,128)(2,1)}), bf16[4,64,1536]{2,1,0:T(8,128)(2,1)S(1)}, u32[]{:S(2)}, u32[]{:S(2)}) async-start(bf16[4,64,1536]{2,1,0:T(8,128)(2,1)} %bitcast.1), calls=%async_computation | async-start | bytes 1572864 | tf_op jit(solution)/shard_map/all_to_all | solution.py:215
  10.0 27.3 %collective-permute-start.13 = (f32[2,4608]{1,0:T(2,128)}, f32[2,4608]{1,0:T(2,128)S(1)}, u32[]{:S(2)}, u32[]{:S(2)}) collective-permute-start(f32[2,4608]{1,0:T(2,128)} %fusion.16), channel_id=1, source_target_pairs={{1,0},{8,9},{17,16},{24,25},{33,32},{40,41},{49,48},{56,57},{65,64... | collective-permute-start | bytes 110600 | tf_op jit(solution)/shard_map/ppermute | solution.py:45
  11.3 93.3 %collective-permute-start.14 = (bf16[768,4608]{1,0:T(8,128)(2,1)}, bf16[768,4608]{1,0:T(8,128)(2,1)}, u32[]{:S(2)}, u32[]{:S(2)}) collective-permute-start(bf16[768,4608]{1,0:T(8,128)(2,1)} %bitcast.79), channel_id=1, source_target_pairs={{1,0},{8,9},{17,16},{24,25},{33,32},{40,41},{49,48},{56,57},{65,64... | collective-permute-start | bytes 21233672 | tf_op jit(solution)/shard_map/ppermute | solution.py:45
  19.5 17.8 %copy-start.2 = (bf16[1,768,1536]{2,1,0:T(8,128)(2,1)S(1)}, bf16[1,768,1536]{2,1,0:T(8,128)(2,1)}, u32[]{:S(2)}) copy-start(bf16[1,768,1536]{2,1,0:T(8,128)(2,1)} %param.17) | copy-start | bytes 7077892
  19.5 19.1 %copy-start.24 = (s32[4,1]{0,1:T(1,128)S(1)}, s32[4,1]{0,1:T(1,128)}, u32[]{:S(2)}) copy-start(s32[4,1]{0,1:T(1,128)} %param.12) | copy-start | bytes 52
  19.5 8.0 %collective-permute-start = (bf16[66,1536]{1,0:T(8,128)(2,1)S(1)}, bf16[66,1536]{1,0:T(8,128)(2,1)S(1)}, u32[]{:S(2)}, u32[]{:S(2)}) collective-permute-start(bf16[66,1536]{1,0:T(8,128)(2,1)S(1)} %pad_maximum_fusion.2), channel_id=1, source_target_pairs={{8,0},{17,9},{10,2},{19,11},{12,4},{21,13},{14,6},{23,15},{88,80},... | collective-permute-start | bytes 608264 | tf_op jit(solution)/shard_map/ppermute | solution.py:45
  20.4 10.6 %collective-permute-start.6 = (bf16[66,1536]{1,0:T(8,128)(2,1)S(1)}, bf16[66,1536]{1,0:T(8,128)(2,1)S(1)}, u32[]{:S(2)}, u32[]{:S(2)}) collective-permute-start(bf16[66,1536]{1,0:T(8,128)(2,1)S(1)} %pad_maximum_fusion.2), channel_id=1, source_target_pairs={{56,0},{1,9},{58,2},{3,11},{60,4},{5,13},{62,6},{7,15},{72,80},{81... | collective-permute-start | bytes 608264 | tf_op jit(solution)/shard_map/ppermute | solution.py:45
  21.1 9.9 %collective-permute-start.5 = (bf16[66,1536]{1,0:T(8,128)(2,1)S(1)}, bf16[66,1536]{1,0:T(8,128)(2,1)S(1)}, u32[]{:S(2)}, u32[]{:S(2)}) collective-permute-start(bf16[66,1536]{1,0:T(8,128)(2,1)S(1)} %pad_maximum_fusion.2), channel_id=1, source_target_pairs={{48,0},{57,9},{50,2},{59,11},{52,4},{61,13},{54,6},{63,15},{64,80}... | collective-permute-start | bytes 608264 | tf_op jit(solution)/shard_map/ppermute | solution.py:45
  27.5 0.7 collective-permute-start.1
  28.2 0.7 collective-permute-start.2
  29.0 0.7 collective-permute-start.3
  29.7 0.7 collective-permute-start.4
  34.0 7.2 %collective-permute-start.8 = (bf16[80,1536]{1,0:T(8,128)(2,1)S(1)}, bf16[80,1536]{1,0:T(8,128)(2,1)S(1)}, u32[]{:S(2)}, u32[]{:S(2)}) collective-permute-start(bf16[80,1536]{1,0:T(8,128)(2,1)S(1)} %pad_maximum_fusion.1), channel_id=1, source_target_pairs={{0,128},{2,130},{4,132},{6,134},{9,137},{11,139},{13,141},{15,143}... | collective-permute-start | bytes 737288 | tf_op jit(solution)/shard_map/ppermute | solution.py:45
  34.6 45.8 %collective-permute-start.7 = (bf16[80,1536]{1,0:T(8,128)(2,1)S(1)}, bf16[80,1536]{1,0:T(8,128)(2,1)S(1)}, u32[]{:S(2)}, u32[]{:S(2)}) collective-permute-start(bf16[80,1536]{1,0:T(8,128)(2,1)S(1)} %pad_maximum_fusion.1), channel_id=1, source_target_pairs={{0,64},{2,66},{4,68},{6,70},{9,73},{11,75},{13,77},{15,79},{80,144... | collective-permute-start | bytes 737288 | tf_op jit(solution)/shard_map/ppermute | solution.py:45
  35.9 45.2 %collective-permute-start.9 = (bf16[80,1536]{1,0:T(8,128)(2,1)S(1)}, bf16[80,1536]{1,0:T(8,128)(2,1)}, u32[]{:S(2)}, u32[]{:S(2)}) collective-permute-start(bf16[80,1536]{1,0:T(8,128)(2,1)S(1)} %pad_maximum_fusion.1), channel_id=1, source_target_pairs={{0,192},{2,194},{4,196},{6,198},{9,201},{11,203},{13,205},{15,207}... | collective-permute-start | bytes 737288 | tf_op jit(solution)/shard_map/ppermute | solution.py:45
  37.3 91.5 %collective-permute-start.15 = (bf16[768,1536]{1,0:T(8,128)(2,1)S(1)}, bf16[768,1536]{1,0:T(8,128)(2,1)}, u32[]{:S(2)}, u32[]{:S(2)}) collective-permute-start(bf16[768,1536]{1,0:T(8,128)(2,1)S(1)} %bitcast.97), channel_id=1, source_target_pairs={{1,0},{8,9},{17,16},{24,25},{33,32},{40,41},{49,48},{56,57},{65,64... | collective-permute-start | bytes 7077896 | tf_op jit(solution)/shard_map/ppermute | solution.py:45
  82.3 11.9 %collective-permute-start.12 = (bf16[80,1536]{1,0:T(8,128)(2,1)S(1)}, bf16[80,1536]{1,0:T(8,128)(2,1)S(1)}, u32[]{:S(2)}, u32[]{:S(2)}) collective-permute-start(bf16[80,1536]{1,0:T(8,128)(2,1)S(1)} %add_add_fusion), channel_id=1, source_target_pairs={{6,0},{15,9},{22,16},{31,25},{38,32},{47,41},{54,48},{63,57},{70,6... | collective-permute-start | bytes 737288 | tf_op jit(solution)/shard_map/ppermute | solution.py:45
  83.6 11.5 %collective-permute-start.11 = (bf16[80,1536]{1,0:T(8,128)(2,1)S(1)}, bf16[80,1536]{1,0:T(8,128)(2,1)}, u32[]{:S(2)}, u32[]{:S(2)}) collective-permute-start(bf16[80,1536]{1,0:T(8,128)(2,1)S(1)} %add_add_fusion), channel_id=1, source_target_pairs={{4,0},{13,9},{20,16},{29,25},{36,32},{45,41},{52,48},{61,57},{68,6... | collective-permute-start | bytes 737288 | tf_op jit(solution)/shard_map/ppermute | solution.py:45
  84.9 11.2 %collective-permute-start.10 = (bf16[80,1536]{1,0:T(8,128)(2,1)S(1)}, bf16[80,1536]{1,0:T(8,128)(2,1)S(1)}, u32[]{:S(2)}, u32[]{:S(2)}) collective-permute-start(bf16[80,1536]{1,0:T(8,128)(2,1)S(1)} %add_add_fusion), channel_id=1, source_target_pairs={{2,0},{11,9},{18,16},{27,25},{34,32},{43,41},{50,48},{59,57},{66,6... | collective-permute-start | bytes 737288 | tf_op jit(solution)/shard_map/ppermute | solution.py:45
  149.2 22.5 %collective-permute-start.16 = (bf16[512,1536]{1,0:T(8,128)(2,1)}, bf16[512,1536]{1,0:T(8,128)(2,1)S(1)}, u32[]{:S(2)}, u32[]{:S(2)}) collective-permute-start(bf16[512,1536]{1,0:T(8,128)(2,1)} %attention.8), channel_id=1, source_target_pairs={{0,64},{9,73},{16,80},{25,89},{32,96},{41,105},{48,112},{57,121}} | collective-permute-start | bytes 4718600 | tf_op jit(solution)/shard_map/ppermute | solution.py:45
  208.7 19.5 %collective-permute-start.17 = (bf16[512,1536]{1,0:T(8,128)(2,1)}, bf16[512,1536]{1,0:T(8,128)(2,1)S(1)}, u32[]{:S(2)}, u32[]{:S(2)}) collective-permute-start(bf16[512,1536]{1,0:T(8,128)(2,1)} %attention.9), channel_id=1, source_target_pairs={{64,128},{73,137},{80,144},{89,153},{96,160},{105,169},{112,176},{... | collective-permute-start | bytes 4718600 | tf_op jit(solution)/shard_map/ppermute | solution.py:45
  265.3 2.3 collective-permute-start.18
  307.8 0.9 collective-permute-start.19
  346.3 45.1 %collective-permute-start.20 = (bf16[512,1536]{1,0:T(8,128)(2,1)}, bf16[512,1536]{1,0:T(8,128)(2,1)S(1)}, u32[]{:S(2)}, u32[]{:S(2)}) collective-permute-start(bf16[512,1536]{1,0:T(8,128)(2,1)} %attention.12), channel_id=1, source_target_pairs={{0,64},{9,73},{16,80},{25,89},{32,96},{41,105},{48,112},{57,121}} | collective-permute-start | bytes 4718600 | tf_op jit(solution)/shard_map/ppermute | solution.py:45
  428.4 19.5 %collective-permute-start.21 = (bf16[512,1536]{1,0:T(8,128)(2,1)}, bf16[512,1536]{1,0:T(8,128)(2,1)S(1)}, u32[]{:S(2)}, u32[]{:S(2)}) collective-permute-start(bf16[512,1536]{1,0:T(8,128)(2,1)} %attention.13), channel_id=1, source_target_pairs={{64,128},{73,137},{80,144},{89,153},{96,160},{105,169},{112,176},{... | collective-permute-start | bytes 4718600 | tf_op jit(solution)/shard_map/ppermute | solution.py:45
  484.9 2.3 collective-permute-start.22
  526.7 48.5 %copy-start.1 = (bf16[1,128,4608]{2,1,0:T(8,128)(2,1)S(1)}, bf16[1,128,4608]{2,1,0:T(8,128)(2,1)}, u32[]{:S(2)}) copy-start(bf16[1,128,4608]{2,1,0:T(8,128)(2,1)} %param.18) | copy-start | bytes 3538948
  527.5 0.7 collective-permute-start.23
  529.2 43.8 %all-to-all-start.1 = ((f32[32,1,1024]{2,1,0:T(1,128)}), f32[32,1,1024]{2,1,0:T(1,128)S(1)}, u32[]{:S(2)}, u32[]{:S(2)}) async-start(f32[32,1,1024]{2,1,0:T(1,128)} %reshape.134), calls=%async_computation.1 | async-start | bytes 262144 | tf_op jit(solution)/shard_map/all_to_all | solution.py:302
  (20 other events, 33.3 us)
